TPU v7x, 512 devices: a whole 4x4x16 slice. The times are simulated.
512 devices in a mesh: row: 16 (over x, y_lo, core), col: 32 (over z, y_hi).
Axes of the slice: x: 4, y: 4 (y_hi: 2, y_lo: 2; y = y_hi * 2 + y_lo), z: 16, core: 2. Of those that a mesh axis runs over, the one named last changes fastest.
Arguments:
- features: bfloat16 [128, 1024, 256], P('row', 'col'), may hold values from -16 to 16
- expand_weight: bfloat16 [2, 256, 1024], replicated, may hold values from -0.375 to 0.375
- expand_bias: float32 [2, 1024], replicated, may hold values from -3 to 3
- depth_weight: float32 [2, 3, 3, 1024], replicated, may hold values from -2 to 2
- depth_bias: float32 [2, 1024], replicated, may hold values from -3 to 3
- project_weight: bfloat16 [2, 1024, 256], replicated, may hold values from -0.1875 to 0.1875
- project_bias: float32 [2, 256], replicated, may hold values from -3 to 3
- qkv_weight: bfloat16 [2, 256, 768], replicated, may hold values from -0.375 to 0.375
- aggregate_depth: float32 [2, 5, 5, 768], replicated, may hold values from -1.25 to 1.25
- aggregate_group: bfloat16 [2, 24, 32, 32], replicated, may hold values from -1 to 1
- output_weight: bfloat16 [2, 512, 256], replicated, may hold values from -0.25 to 0.25
- output_bias: float32 [2, 256], replicated, may hold values from -3 to 3
- head_weight: bfloat16 [3, 3, 4, 256], replicated, may hold values from -0.125 to 0.125
- head_bias: float32 [4], replicated, may hold values from -3 to 3
Outputs:
- final_map: bfloat16 [128, 1024, 256], P('row', 'col')
- boxes: float32 [4, 128, 1024], P(None, 'row', 'col')
All inputs are finite; a program needn't handle non-finite values.
Results may differ from a plain program's by a relative error of at most 0.009.
Values may be sent and summed in bfloat16 or wider, within the bound.
A program may use at most 64 MiB of HBM per device.

v0:
```python
import jax
import jax.numpy as jnp
from jax import lax
from jax.sharding import PartitionSpec as P

SECTIONS = 2


def with_halo(cells, sides, width):
    for axis, dim in sides:
        count = lax.axis_size(axis)
        ends = count - 1
        head = lax.slice_in_dim(cells, 0, width, axis=dim)
        tail = lax.slice_in_dim(cells, cells.shape[dim] - width, cells.shape[dim], axis=dim)
        cells = jnp.concatenate(
            [
                lax.ppermute(tail, axis, [(i, (i + 1) % count) for i in range(ends)]),
                cells,
                lax.ppermute(head, axis, [((i + 1) % count, i) for i in range(ends)]),
            ],
            axis=dim,
        )
    return cells


def hard_swish(value):
    return value * jnp.minimum(jnp.maximum(value + 3.0, 0.0), 6.0) / 6.0


def depthwise(padded, weight, rows, cols):
    ksize = weight.shape[0]
    total = jnp.zeros((rows, cols, padded.shape[2]), jnp.float32)
    for offset_r in range(ksize):
        for offset_c in range(ksize):
            total = (
                total
                + padded[offset_r : offset_r + rows, offset_c : offset_c + cols, :].astype(
                    jnp.float32
                )
                * weight[offset_r, offset_c]
            )
    return total


def dense(values, weight):
    return lax.dot_general(
        values, weight, (((values.ndim - 1,), (0,)), ((), ())), preferred_element_type=jnp.float32
    )


def heads_of(padded_qkv, agg_depth, agg_group, rows, cols, heads, head_dim):
    center = padded_qkv[2 : 2 + rows, 2 : 2 + cols, :]
    spread = depthwise(padded_qkv, agg_depth, rows, cols).astype(jnp.bfloat16)
    grouped = jnp.einsum(
        "rcgd,gde->rcge",
        spread.reshape(rows, cols, 3 * heads, head_dim),
        agg_group,
        preferred_element_type=jnp.float32,
    ).astype(jnp.bfloat16)
    return jnp.concatenate(
        [
            center.reshape(rows, cols, heads, 3, head_dim),
            grouped.reshape(rows, cols, heads, 3, head_dim),
        ],
        axis=2,
    )


def local(
    features,
    expand_weight,
    expand_bias,
    depth_weight,
    depth_bias,
    project_weight,
    project_bias,
    qkv_weight,
    aggregate_depth,
    aggregate_group,
    output_weight,
    output_bias,
    head_weight,
    head_bias,
):
    rows, cols, width = features.shape
    head_dim = aggregate_group.shape[2]
    heads = width // head_dim
    current = features
    for section in range(SECTIONS):
        hidden = hard_swish(dense(current, expand_weight[section]) + expand_bias[section]).astype(
            jnp.bfloat16
        )
        hidden = with_halo(hidden, (("row", 0), ("col", 1)), 1)
        spread = hard_swish(
            depthwise(hidden, depth_weight[section], rows, cols) + depth_bias[section]
        ).astype(jnp.bfloat16)
        mixed = (current + dense(spread, project_weight[section]) + project_bias[section]).astype(
            jnp.bfloat16
        )
        local_qkv = dense(mixed, qkv_weight[section]).astype(jnp.bfloat16)
        padded_qkv = with_halo(local_qkv, (("row", 0), ("col", 1)), 2)
        both = heads_of(
            padded_qkv,
            aggregate_depth[section],
            aggregate_group[section],
            rows,
            cols,
            heads,
            head_dim,
        )
        queries = jax.nn.relu(both[:, :, :, 0, :]).astype(jnp.float32)
        keys = jax.nn.relu(both[:, :, :, 1, :]).astype(jnp.float32)
        values = both[:, :, :, 2, :].astype(jnp.float32)
        kv_local = jnp.einsum("rchd,rche->hde", keys, values, precision=lax.Precision.HIGHEST)
        key_local = jnp.sum(keys, axis=(0, 1))
        kv_all, key_all = lax.psum((kv_local, key_local), ("row", "col"))
        numer = jnp.einsum("rchd,hde->rche", queries, kv_all, precision=lax.Precision.HIGHEST)
        denom = jnp.einsum("rchd,hd->rch", queries, key_all, precision=lax.Precision.HIGHEST)
        attended = (
            (numer / (denom[..., None] + 1e-06)).astype(jnp.bfloat16).reshape(rows, cols, 2 * width)
        )
        current = (mixed + dense(attended, output_weight[section]) + output_bias[section]).astype(
            jnp.bfloat16
        )
    padded = with_halo(current, (("row", 0), ("col", 1)), 1)
    boxes = jnp.zeros((4, rows, cols), jnp.float32)
    for offset_r in range(3):
        for offset_c in range(3):
            window = padded[offset_r : offset_r + rows, offset_c : offset_c + cols, :]
            boxes = boxes + lax.dot_general(
                head_weight[offset_r, offset_c],
                window,
                (((1,), (2,)), ((), ())),
                preferred_element_type=jnp.float32,
            )
    boxes = boxes + head_bias[:, None, None]
    return (current, boxes)


def solution(mesh):
    return jax.shard_map(
        local,
        mesh=mesh,
        in_specs=(
            P("row", "col", None),
            P(),
            P(),
            P(),
            P(),
            P(),
            P(),
            P(),
            P(),
            P(),
            P(),
            P(),
            P(),
            P(),
        ),
        out_specs=(P("row", "col", None), P(None, "row", "col")),
        check_vma=False,
    )
```

profile of v0, /device:TPU:1, one launch (start us, length us, event | category | flops | bytes accessed | tf_op | source)
XLA Modules:
  0.0 1291.3 jit_solution(16654592046291332820)
XLA Ops:
  7.3 1.4 fusion.129
  8.6 1.5 multiply_convert_fusion.3
  10.1 4.6 collective-permute-start
  14.7 5.5 collective-permute-start.1
  21.7 0.7 copy_bitcast_fusion
  23.1 1.9 collective-permute-start.2
  24.9 1.3 collective-permute-start.3
  26.2 0.7 slice_reduce_fusion.49
  27.0 4.2 collective-permute-done.3
  31.6 1.5 fusion.11
  33.4 0.7 fusion.122
  34.1 3.7 collective-permute-start.4
  37.8 1.9 collective-permute-start.5
  39.7 0.6 slice_reduce_fusion.48
  40.4 1.6 reshape.49
  42.0 2.0 collective-permute-done.5
  44.0 6.0 collective-permute-start.6
  50.0 1.3 collective-permute-start.7
  51.3 1.9 copy_dynamic-update-slice_fusion.3
  53.3 2.9 collective-permute-done.7
  56.7 3.0 add_convert_fusion.1
  59.7 1.1 reshape.50
  61.3 1.3 copy-done
  63.4 1.4 copy-done.1
  64.8 1.1 convolution_bitcast_fusion.1
  66.0 111.1 %psum.29 = f32[16,32]{1,0:T(8,128)S(1)} all-reduce(f32[16,32]{1,0:T(8,128)S(1)} %convert_reduce_fusion.1), channel_id=1, replica_groups=mesh['row'=16,'col'=32] {'row','col'}, use_global_device_ids=true, to_apply=%region_2.3 | all-reduce | flops 512 | bytes 4096 | tf_op jit(solution)/shard_map/psum | solution.py:116
  177.0 5.4 fusion.26
  182.5 450.1 %all-reduce.3.cloned.1.call-done = f32[16,32,32]{1,2,0:T(8,128)} async-done(((f32[16,32,32]{1,2,0:T(8,128)}), f32[16,32,32]{1,2,0:T(8,128)}) %all-reduce.3.cloned.1.call-update) | async-done | bytes 65552 | tf_op jit(solution)/shard_map/psum | solution.py:116
  632.6 6.1 fusion.1
  638.7 1.0 copy.25
  639.7 1.0 reshape.52
  640.8 1.2 fusion.8
  642.4 4.9 collective-permute-start.8
  647.3 1.9 collective-permute-start.9
  649.3 3.6 collective-permute-done.9
  653.0 4.5 collective-permute-start.10
  657.5 1.3 collective-permute-start.11
  658.9 4.8 collective-permute-done.11
  664.1 1.5 fusion.10
  666.0 2.7 collective-permute-start.12
  668.7 1.9 collective-permute-start.13
  670.7 1.6 reshape.53
  672.3 2.3 collective-permute-done.13
  674.7 3.1 collective-permute-start.14
  677.8 1.5 collective-permute-start.15
  679.3 1.9 copy_dynamic-update-slice_fusion.1
  681.2 2.8 collective-permute-done.15
  684.3 3.0 add_convert_fusion
  687.3 1.1 reshape.54
  689.0 1.3 copy-done.2
  691.1 1.4 copy-done.3
  692.4 1.1 convolution_bitcast_fusion
  693.6 105.8 %psum.31 = f32[16,32]{1,0:T(8,128)S(1)} all-reduce(f32[16,32]{1,0:T(8,128)S(1)} %convert_reduce_fusion), channel_id=1, replica_groups=mesh['row'=16,'col'=32] {'row','col'}, use_global_device_ids=true, to_apply=%region_5.6 | all-reduce | flops 512 | bytes 4096 | tf_op jit(solution)/shard_map/psum | solution.py:116
  799.4 5.4 fusion.29
  804.9 448.7 %all-reduce.5.cloned.1.call-done = f32[16,32,32]{1,2,0:T(8,128)} async-done(((f32[16,32,32]{1,2,0:T(8,128)}), f32[16,32,32]{1,2,0:T(8,128)}) %all-reduce.5.cloned.1.call-update) | async-done | bytes 65552 | tf_op jit(solution)/shard_map/psum | solution.py:116
  1253.6 6.1 fusion
  1259.8 1.0 copy.31
  1260.8 1.0 reshape.56
  1262.1 4.9 collective-permute-start.16
  1267.0 1.9 collective-permute-start.17
  1269.2 2.9 collective-permute-done.17
  1272.1 4.5 collective-permute-start.18
  1276.6 1.3 collective-permute-start.19
  1278.3 4.2 collective-permute-done.19
  (151 shorter events, 10.5 us)
Async XLA Ops:
  7.2 13.1 %copy-start.35 = (f32[2,256]{1,0:T(2,128)S(1)}, f32[2,256]{1,0:T(2,128)}, u32[]{:S(2)}) copy-start(f32[2,256]{1,0:T(2,128)} %param.20) | copy-start | bytes 6148
  7.2 13.7 %copy-start.32 = (f32[2,1024]{1,0:T(2,128)S(1)}, f32[2,1024]{1,0:T(2,128)}, u32[]{:S(2)}) copy-start(f32[2,1024]{1,0:T(2,128)} %param.18) | copy-start | bytes 24580
  7.2 14.3 %copy-start.14 = (f32[2,3,3,1024]{3,0,2,1:T(2,128)S(1)}, f32[2,3,3,1024]{3,0,2,1:T(2,128)}, u32[]{:S(2)}) copy-start(f32[2,3,3,1024]{3,0,2,1:T(2,128)} %param.17) | copy-start | bytes 221188
  7.2 14.4 %copy-start.9 = (f32[2,5,5,768]{3,0,2,1:T(2,128)S(1)}, f32[2,5,5,768]{3,0,2,1:T(2,128)}, u32[]{:S(2)}) copy-start(f32[2,5,5,768]{3,0,2,1:T(2,128)} %param.22) | copy-start | bytes 460804
  7.2 625.4 %all-reduce.3.cloned.1.call-start = ((), (), s32[]{:S(2)}) async-start(), calls=%async_computation | async-start | bytes 524288 | tf_op jit(solution)/shard_map/psum | solution.py:116
  8.6 13.8 %copy-start.36 = (f32[2,256]{1,0:T(2,128)S(1)}, f32[2,256]{1,0:T(2,128)}, u32[]{:S(2)}) copy-start(f32[2,256]{1,0:T(2,128)} %param.25) | copy-start | bytes 6148
  10.1 12.8 collective-permute-start
  14.7 8.2 collective-permute-start.1
  23.0 8.6 copy-start.42
  23.0 8.6 copy-start.45
  23.1 3.9 collective-permute-start.2
  24.9 6.3 collective-permute-start.3
  33.1 6.6 copy-start.10
  34.1 7.9 collective-permute-start.4
  37.8 6.1 collective-permute-start.5
  44.0 9.3 collective-permute-start.6
  50.0 6.2 collective-permute-start.7
  53.2 3.3 copy-start.15
  53.2 3.3 copy-start.16
  53.2 3.3 copy-start.17
  53.2 3.4 copy-start.18
  53.2 3.4 copy-start.19
  53.2 3.4 copy-start.20
  53.2 3.4 copy-start.21
  53.2 3.4 copy-start.22
  53.2 3.4 copy-start.23
  53.2 3.4 copy-start.24
  53.3 3.4 copy-start.25
  53.3 3.4 copy-start.26
  53.3 3.4 copy-start.27
  53.3 3.4 copy-start.28
  53.3 3.4 copy-start.29
  53.3 3.4 copy-start.30
  53.3 3.4 copy-start.31
  60.8 1.9 copy-start
  182.4 1071.2 %all-reduce.5.cloned.1.call-start = ((), (), s32[]{:S(2)}) async-start(), calls=%async_computation.1 | async-start | bytes 524288 | tf_op jit(solution)/shard_map/psum | solution.py:116
  638.7 2.0 copy-start.11
  638.7 2.0 copy-start.39
  638.7 3.2 copy-start.34
  639.7 2.2 copy-start.41
  642.0 16.8 %copy-start.8 = (f32[5,5,768]{2,1,0:T(8,128)S(1)}, f32[5,5,768]{2,1,0:T(8,128)}, u32[]{:S(2)}) copy-start(f32[5,5,768]{2,1,0:T(8,128)} %get-tuple-element.118) | copy-start | bytes 230404
  642.4 7.0 collective-permute-start.8
  647.3 5.6 collective-permute-start.9
  649.3 14.8 %copy-start.33 = (f32[1,1024]{1,0:T(1,128)S(1)}, f32[1,1024]{1,0:T(1,128)}, u32[]{:S(2)}) copy-start(f32[1,1024]{1,0:T(1,128)} %get-tuple-element.108) | copy-start | bytes 12292
  649.3 14.8 %copy-start.38 = (f32[1,256]{1,0:T(1,128)S(1)}, f32[1,256]{1,0:T(1,128)}, u32[]{:S(2)}) copy-start(f32[1,256]{1,0:T(1,128)} %get-tuple-element.114) | copy-start | bytes 3076
  649.3 14.8 %copy-start.43 = (bf16[2,1024,256]{2,1,0:T(8,128)(2,1)S(1)}, bf16[2,1024,256]{2,1,0:T(8,128)(2,1)}, u32[]{:S(2)}) copy-start(bf16[2,1024,256]{2,1,0:T(8,128)(2,1)} %param.19) | copy-start | bytes 3145732
  653.0 6.0 collective-permute-start.10
  657.5 6.3 collective-permute-start.11
  665.6 5.0 copy-start.12
  666.0 6.3 collective-permute-start.12
  668.7 5.9 collective-permute-start.13
  674.7 6.6 collective-permute-start.14
  677.8 6.2 collective-permute-start.15
  688.4 1.9 copy-start.2
  1259.7 2.0 copy-start.13
  1259.8 2.0 copy-start.37
  1259.8 2.0 copy-start.44
  1259.8 9.2 copy-start.40
  1261.8 21.8 %copy-start.46 = (f32[4]{0:T(128)S(1)}, f32[4]{0:T(128)}, u32[]{:S(2)}) copy-start(f32[4]{0:T(128)} %param.27) | copy-start | bytes 52
  1262.0 22.4 %copy-start.4 = (bf16[8,32,256]{2,1,0:T(8,128)(2,1)}, bf16[8,32,256]{2,1,0:T(8,128)(2,1)S(1)}, u32[]{:S(2)}) copy-start(bf16[8,32,256]{2,1,0:T(8,128)(2,1)S(1)} %fusion.9) | copy-start | bytes 393220
  1262.1 7.1 collective-permute-start.16
  1267.0 5.1 collective-permute-start.17
  1272.1 6.2 collective-permute-start.18
  1276.6 5.9 collective-permute-start.19
  (5 other events, 7.0 us)
Sparse Core Ops, SparseCore 0:
  182.6 449.9 all-reduce.2
  805.0 448.5 all-reduce.4
where the time goes:
time: 1290 us
  waiting for transfers between devices  929 us (72%)
  blocking collectives  217 us (17%)
  starting transfers between devices  60.7 us (5%)
  matrix products  35 us (3%)
  local copies, waits for them, and re-layouts  26.6 us (2%)
  between operations  15.2 us (1%)
    psum x2, waiting for transfers between devices, local(): kv_all, key_all = lax.psum((kv_local, key_local), ('row', 'col'))  899 us
    psum x2, blocking collectives, local(): kv_all, key_all = lax.psum((kv_local, key_local), ('row', 'col'))  217 us
    ppermute x10, starting transfers between devices, with_halo(): lax.ppermute(tail, axis, [(i, (i + 1) % count) for i in range(ends)])  40.8 us
    ppermute x10, waiting for transfers between devices, with_halo(): lax.ppermute(head, axis, [((i + 1) % count, i) for i in range(ends)])  29.7 us
  transfers between devices with their start and end apart: 22, of which 11 were waited for; matrix products, arithmetic and copies ran while one was open for 1% of the time, Pallas kernels for 0%

commit v1 on v0

--- a/solution.py
+++ b/solution.py
@@ -4,6 +4,11 @@
 from jax.sharding import PartitionSpec as P
 
 SECTIONS = 2
+
+
+def one_after_other(value_2, one, other):
+    partial = lax.psum(value_2, one)
+    return lax.psum(partial, other)
 
 
 def with_halo(cells, sides, width):
@@ -113,7 +118,7 @@
         values = both[:, :, :, 2, :].astype(jnp.float32)
         kv_local = jnp.einsum("rchd,rche->hde", keys, values, precision=lax.Precision.HIGHEST)
         key_local = jnp.sum(keys, axis=(0, 1))
-        kv_all, key_all = lax.psum((kv_local, key_local), ("row", "col"))
+        kv_all, key_all = one_after_other((kv_local, key_local), "row", "col")
         numer = jnp.einsum("rchd,hde->rche", queries, kv_all, precision=lax.Precision.HIGHEST)
         denom = jnp.einsum("rchd,hd->rch", queries, key_all, precision=lax.Precision.HIGHEST)
         attended = (

time: 1290 us -> 1250 us (0.969)
  waiting for transfers between devices: 929 us -> 885 us
  starting transfers between devices: 60.7 us -> 95.9 us
  blocking collectives: 217 us -> 183 us
    psum x2 -> x4, waiting for transfers between devices: 899 us -> 855 us  [the longest x2 580 us: one_after_other(): return lax.psum(partial, other)]
    ppermute x10, starting transfers between devices: 40.8 us -> 75.5 us  [with_halo(): lax.ppermute(tail, axis, [(i, (i + 1) % count) for i in range(ends)])]
    psum x2 -> x4, blocking collectives: 217 us -> 183 us  [the longest x2 130 us: one_after_other(): return lax.psum(partial, other)]
  transfers between devices with their start and end apart: 22 -> 24, of which waited for: 11 -> 13; matrix products, arithmetic and copies ran while one was open for 1% -> 2% of each run, Pallas kernels for 0% -> 0%
where the time goes in v1:
time: 1250 us
  waiting for transfers between devices  885 us (71%)
  blocking collectives  183 us (15%)
  starting transfers between devices  95.9 us (8%)
  matrix products  35 us (3%)
  local copies, waits for them, and re-layouts  26.6 us (2%)
  between operations  15 us (1%)
    psum x2, waiting for transfers between devices, one_after_other(): return lax.psum(partial, other)  580 us
    psum x2, waiting for transfers between devices, one_after_other(): partial = lax.psum(value_2, one)  275 us
    psum x2, blocking collectives, one_after_other(): return lax.psum(partial, other)  130 us
    ppermute x10, starting transfers between devices, with_halo(): lax.ppermute(tail, axis, [(i, (i + 1) % count) for i in range(ends)])  75.5 us
    psum x2, blocking collectives, one_after_other(): partial = lax.psum(value_2, one)  52.7 us
    ppermute x10, waiting for transfers between devices, with_halo(): lax.ppermute(head, axis, [((i + 1) % count, i) for i in range(ends)])  29.7 us
  transfers between devices with their start and end apart: 24, of which 13 were waited for; matrix products, arithmetic and copies ran while one was open for 2% of the time, Pallas kernels for 0%

profile of v1, /device:TPU:1, one launch (start us, length us, event | category | flops | bytes accessed | tf_op | source)
XLA Modules:
  0.0 1248.6 jit_solution(2628014274538968885)
XLA Ops:
  7.3 1.4 fusion.129
  8.6 1.5 multiply_convert_fusion.3
  10.1 4.6 collective-permute-start
  14.7 5.5 collective-permute-start.1
  23.1 1.9 collective-permute-start.2
  24.9 1.3 collective-permute-start.3
  27.0 4.2 collective-permute-done.3
  31.6 1.5 fusion.11
  34.1 3.7 collective-permute-start.4
  37.8 1.9 collective-permute-start.5
  40.4 1.6 reshape.49
  42.0 2.0 collective-permute-done.5
  44.0 6.0 collective-permute-start.6
  50.0 1.3 collective-permute-start.7
  51.3 1.9 copy_dynamic-update-slice_fusion.3
  53.3 2.9 collective-permute-done.7
  56.7 3.0 add_convert_fusion.1
  59.7 1.1 reshape.50
  61.3 1.3 copy-done
  63.4 1.4 copy-done.1
  64.8 1.1 convolution_bitcast_fusion.1
  66.0 26.4 %psum.58 = f32[16,32]{1,0:T(8,128)S(1)} all-reduce(f32[16,32]{1,0:T(8,128)S(1)} %convert_reduce_fusion.1), channel_id=1, replica_groups=mesh['row'=16,'col'=32] {'row'}, use_global_device_ids=true, to_apply=%region_3.4 | all-reduce | flops 512 | bytes 4096 | tf_op jit(solution)/shard_map/psum | solution.py:10
  92.3 68.7 %psum.59 = f32[16,32]{1,0:T(8,128)S(1)} all-reduce(f32[16,32]{1,0:T(8,128)S(1)} %psum.58), channel_id=1, replica_groups=mesh['row'=16,'col'=32] {'col'}, use_global_device_ids=true, to_apply=%region_4.5 | all-reduce | flops 512 | bytes 4096 | tf_op jit(solution)/shard_map/psum | solution.py:11
  161.3 5.4 fusion.26
  166.7 136.4 %all-reduce.5.cloned.1.call-done = f32[16,32,32]{1,2,0:T(8,128)} async-done(((f32[16,32,32]{1,2,0:T(8,128)}), f32[16,32,32]{1,2,0:T(8,128)}) %all-reduce.5.cloned.1.call-update) | async-done | bytes 65552 | tf_op jit(solution)/shard_map/psum | solution.py:10
  303.1 290.3 %all-reduce.7.cloned.1.call-done = f32[16,32,32]{1,2,0:T(8,128)} async-done(((f32[16,32,32]{1,2,0:T(8,128)}), f32[16,32,32]{1,2,0:T(8,128)}) %all-reduce.7.cloned.1.call-update) | async-done | bytes 65552 | tf_op jit(solution)/shard_map/psum | solution.py:11
  593.4 6.1 fusion.1
  599.6 1.0 copy.25
  600.6 1.0 reshape.52
  601.6 1.2 fusion.8
  603.2 22.5 %collective-permute-start.8 = (bf16[1,32,1024]{2,1,0:T(8,128)(2,1)S(1)}, bf16[1,32,1024]{2,1,0:T(8,128)(2,1)S(1)}, u32[]{:S(2)}, u32[]{:S(2)}) collective-permute-start(bf16[1,32,1024]{2,1,0:T(8,128)(2,1)S(1)} %get-tuple-element.72), channel_id=1, source_target_pairs={{0,32},{32,64},{64,96},{96,128},{128,160},{160,192},{192,224},{224... | collective-permute-start | bytes 196616 | tf_op jit(solution)/shard_map/ppermute | solution.py:22
  625.7 1.9 collective-permute-start.9
  627.7 3.6 collective-permute-done.9
  631.4 3.1 collective-permute-start.10
  634.4 1.3 collective-permute-start.11
  635.9 4.8 collective-permute-done.11
  641.1 1.5 fusion.10
  642.9 2.7 collective-permute-start.12
  645.6 1.9 collective-permute-start.13
  647.6 1.6 reshape.53
  649.2 2.3 collective-permute-done.13
  651.6 5.5 collective-permute-start.14
  657.1 1.5 collective-permute-start.15
  658.7 1.9 copy_dynamic-update-slice_fusion.1
  660.5 2.8 collective-permute-done.15
  663.7 3.0 add_convert_fusion
  666.7 1.1 reshape.54
  668.3 1.3 copy-done.2
  670.4 1.4 copy-done.3
  671.8 1.1 convolution_bitcast_fusion
  672.9 26.3 %psum.62 = f32[16,32]{1,0:T(8,128)S(1)} all-reduce(f32[16,32]{1,0:T(8,128)S(1)} %convert_reduce_fusion), channel_id=1, replica_groups=mesh['row'=16,'col'=32] {'row'}, use_global_device_ids=true, to_apply=%region_8.9 | all-reduce | flops 512 | bytes 4096 | tf_op jit(solution)/shard_map/psum | solution.py:10
  699.2 61.8 %psum.63 = f32[16,32]{1,0:T(8,128)S(1)} all-reduce(f32[16,32]{1,0:T(8,128)S(1)} %psum.62), channel_id=1, replica_groups=mesh['row'=16,'col'=32] {'col'}, use_global_device_ids=true, to_apply=%region_9.10 | all-reduce | flops 512 | bytes 4096 | tf_op jit(solution)/shard_map/psum | solution.py:11
  761.3 5.4 fusion.29
  766.7 138.2 %all-reduce.9.cloned.1.call-done = f32[16,32,32]{1,2,0:T(8,128)} async-done(((f32[16,32,32]{1,2,0:T(8,128)}), f32[16,32,32]{1,2,0:T(8,128)}) %all-reduce.9.cloned.1.call-update) | async-done | bytes 65552 | tf_op jit(solution)/shard_map/psum | solution.py:10
  905.0 290.2 %all-reduce.11.cloned.1.call-done = f32[16,32,32]{1,2,0:T(8,128)} async-done(((f32[16,32,32]{1,2,0:T(8,128)}), f32[16,32,32]{1,2,0:T(8,128)}) %all-reduce.11.cloned.1.call-update) | async-done | bytes 65552 | tf_op jit(solution)/shard_map/psum | solution.py:11
  1195.1 6.1 fusion
  1201.3 1.0 copy.31
  1202.3 1.0 reshape.56
  1203.6 22.5 %collective-permute-start.16 = (bf16[1,32,256]{2,1,0:T(8,128)(2,1)S(1)}, bf16[1,32,256]{2,1,0:T(8,128)(2,1)S(1)}, u32[]{:S(2)}, u32[]{:S(2)}) collective-permute-start(bf16[1,32,256]{2,1,0:T(8,128)(2,1)S(1)} %get-tuple-element.86), channel_id=1, source_target_pairs={{0,32},{32,64},{64,96},{96,128},{128,160},{160,192},{192,224},{224... | collective-permute-start | bytes 49160 | tf_op jit(solution)/shard_map/ppermute | solution.py:22
  1226.1 1.9 collective-permute-start.17
  1228.2 2.9 collective-permute-done.17
  1231.2 3.1 collective-permute-start.18
  1234.3 1.3 collective-permute-start.19
  1235.9 4.2 collective-permute-done.19
  (159 shorter events, 13.8 us)
Async XLA Ops:
  7.2 13.1 %copy-start.35 = (f32[2,256]{1,0:T(2,128)S(1)}, f32[2,256]{1,0:T(2,128)}, u32[]{:S(2)}) copy-start(f32[2,256]{1,0:T(2,128)} %param.20) | copy-start | bytes 6148
  7.2 13.7 %copy-start.32 = (f32[2,1024]{1,0:T(2,128)S(1)}, f32[2,1024]{1,0:T(2,128)}, u32[]{:S(2)}) copy-start(f32[2,1024]{1,0:T(2,128)} %param.18) | copy-start | bytes 24580
  7.2 14.3 %copy-start.14 = (f32[2,3,3,1024]{3,0,2,1:T(2,128)S(1)}, f32[2,3,3,1024]{3,0,2,1:T(2,128)}, u32[]{:S(2)}) copy-start(f32[2,3,3,1024]{3,0,2,1:T(2,128)} %param.17) | copy-start | bytes 221188
  7.2 14.4 %copy-start.9 = (f32[2,5,5,768]{3,0,2,1:T(2,128)S(1)}, f32[2,5,5,768]{3,0,2,1:T(2,128)}, u32[]{:S(2)}) copy-start(f32[2,5,5,768]{3,0,2,1:T(2,128)} %param.22) | copy-start | bytes 460804
  7.2 295.8 %all-reduce.5.cloned.1.call-start = ((), (), s32[]{:S(2)}) async-start(), calls=%async_computation | async-start | bytes 524288 | tf_op jit(solution)/shard_map/psum | solution.py:10
  8.6 13.8 %copy-start.36 = (f32[2,256]{1,0:T(2,128)S(1)}, f32[2,256]{1,0:T(2,128)}, u32[]{:S(2)}) copy-start(f32[2,256]{1,0:T(2,128)} %param.25) | copy-start | bytes 6148
  10.1 12.8 %collective-permute-start = (bf16[1,32,1024]{2,1,0:T(8,128)(2,1)S(1)}, bf16[1,32,1024]{2,1,0:T(8,128)(2,1)S(1)}, u32[]{:S(2)}, u32[]{:S(2)}) collective-permute-start(bf16[1,32,1024]{2,1,0:T(8,128)(2,1)S(1)} %get-tuple-element.74), channel_id=1, source_target_pairs={{0,32},{32,64},{64,96},{96,128},{128,160},{160,192},{192,224},{224... | collective-permute-start | bytes 196616 | tf_op jit(solution)/shard_map/ppermute | solution.py:22
  14.7 8.2 collective-permute-start.1
  23.0 8.6 copy-start.42
  23.0 8.6 copy-start.45
  23.1 3.9 collective-permute-start.2
  24.9 6.3 collective-permute-start.3
  33.1 6.6 copy-start.10
  34.1 7.9 collective-permute-start.4
  37.8 6.1 collective-permute-start.5
  44.0 9.3 collective-permute-start.6
  50.0 6.2 collective-permute-start.7
  53.2 3.3 copy-start.15
  53.2 3.3 copy-start.16
  53.2 3.3 copy-start.17
  53.2 3.4 copy-start.18
  53.2 3.4 copy-start.19
  53.2 3.4 copy-start.20
  53.2 3.4 copy-start.21
  53.2 3.4 copy-start.22
  53.2 3.4 copy-start.23
  53.2 3.4 copy-start.24
  53.3 3.4 copy-start.25
  53.3 3.4 copy-start.26
  53.3 3.4 copy-start.27
  53.3 3.4 copy-start.28
  53.3 3.4 copy-start.29
  53.3 3.4 copy-start.30
  53.3 3.4 copy-start.31
  161.1 432.3 %all-reduce.7.cloned.1.call-start = ((), (), s32[]{:S(2)}) async-start(), calls=%async_computation.1 | async-start | bytes 524288 | tf_op jit(solution)/shard_map/psum | solution.py:11
  303.1 601.9 %all-reduce.9.cloned.1.call-start = ((), (), s32[]{:S(2)}) async-start(), calls=%async_computation.2 | async-start | bytes 524288 | tf_op jit(solution)/shard_map/psum | solution.py:10
  599.5 2.0 copy-start.11
  599.5 2.0 copy-start.39
  599.5 3.2 copy-start.34
  600.5 2.2 copy-start.41
  602.8 32.9 %copy-start.8 = (f32[5,5,768]{2,1,0:T(8,128)S(1)}, f32[5,5,768]{2,1,0:T(8,128)}, u32[]{:S(2)}) copy-start(f32[5,5,768]{2,1,0:T(8,128)} %get-tuple-element.118) | copy-start | bytes 230404
  603.2 24.5 %collective-permute-start.8 = (bf16[1,32,1024]{2,1,0:T(8,128)(2,1)S(1)}, bf16[1,32,1024]{2,1,0:T(8,128)(2,1)S(1)}, u32[]{:S(2)}, u32[]{:S(2)}) collective-permute-start(bf16[1,32,1024]{2,1,0:T(8,128)(2,1)S(1)} %get-tuple-element.72), channel_id=1, source_target_pairs={{0,32},{32,64},{64,96},{96,128},{128,160},{160,192},{192,224},{224... | collective-permute-start | bytes 196616 | tf_op jit(solution)/shard_map/ppermute | solution.py:22
  625.7 5.6 collective-permute-start.9
  627.7 13.4 %copy-start.33 = (f32[1,1024]{1,0:T(1,128)S(1)}, f32[1,1024]{1,0:T(1,128)}, u32[]{:S(2)}) copy-start(f32[1,1024]{1,0:T(1,128)} %get-tuple-element.108) | copy-start | bytes 12292
  627.7 13.4 %copy-start.38 = (f32[1,256]{1,0:T(1,128)S(1)}, f32[1,256]{1,0:T(1,128)}, u32[]{:S(2)}) copy-start(f32[1,256]{1,0:T(1,128)} %get-tuple-element.114) | copy-start | bytes 3076
  627.7 13.4 %copy-start.43 = (bf16[2,1024,256]{2,1,0:T(8,128)(2,1)S(1)}, bf16[2,1024,256]{2,1,0:T(8,128)(2,1)}, u32[]{:S(2)}) copy-start(bf16[2,1024,256]{2,1,0:T(8,128)(2,1)} %param.19) | copy-start | bytes 3145732
  631.4 4.5 collective-permute-start.10
  634.4 6.3 collective-permute-start.11
  642.6 5.0 copy-start.12
  642.9 6.3 collective-permute-start.12
  645.6 5.9 collective-permute-start.13
  651.6 8.9 collective-permute-start.14
  657.1 6.2 collective-permute-start.15
  761.0 434.1 %all-reduce.11.cloned.1.call-start = ((), (), s32[]{:S(2)}) async-start(), calls=%async_computation.3 | async-start | bytes 524288 | tf_op jit(solution)/shard_map/psum | solution.py:11
  1201.3 2.0 copy-start.13
  1201.3 2.0 copy-start.37
  1201.3 2.0 copy-start.44
  1201.3 26.7 %copy-start.40 = (bf16[3,3,4,256]{3,2,1,0:T(4,128)(2,1)S(1)}, bf16[3,3,4,256]{3,2,1,0:T(4,128)(2,1)}, u32[]{:S(2)}) copy-start(bf16[3,3,4,256]{3,2,1,0:T(4,128)(2,1)} %param.26) | copy-start | bytes 55300
  1203.3 37.9 %copy-start.46 = (f32[4]{0:T(128)S(1)}, f32[4]{0:T(128)}, u32[]{:S(2)}) copy-start(f32[4]{0:T(128)} %param.27) | copy-start | bytes 52
  1203.6 38.5 %copy-start.4 = (bf16[8,32,256]{2,1,0:T(8,128)(2,1)}, bf16[8,32,256]{2,1,0:T(8,128)(2,1)S(1)}, u32[]{:S(2)}) copy-start(bf16[8,32,256]{2,1,0:T(8,128)(2,1)S(1)} %fusion.9) | copy-start | bytes 393220
  1203.6 24.6 %collective-permute-start.16 = (bf16[1,32,256]{2,1,0:T(8,128)(2,1)S(1)}, bf16[1,32,256]{2,1,0:T(8,128)(2,1)S(1)}, u32[]{:S(2)}, u32[]{:S(2)}) collective-permute-start(bf16[1,32,256]{2,1,0:T(8,128)(2,1)S(1)} %get-tuple-element.86), channel_id=1, source_target_pairs={{0,32},{32,64},{64,96},{96,128},{128,160},{160,192},{192,224},{224... | collective-permute-start | bytes 49160 | tf_op jit(solution)/shard_map/ppermute | solution.py:22
  1226.1 5.1 collective-permute-start.17
  1231.2 4.8 collective-permute-start.18
  1234.3 5.9 collective-permute-start.19
  (7 other events, 10.8 us)
Sparse Core Ops, SparseCore 0:
  161.2 141.8 all-reduce.4
  306.2 287.1 all-reduce.6
  761.1 143.7 all-reduce.8
  907.9 287.1 all-reduce.10
